TPU v7x, 32 devices: a whole 2x2x4 slice. The times are simulated.
32 devices in a mesh: row: 8 (over y, x, core), col: 4 (over z).
Axes of the slice: x: 2, y: 2, z: 4, core: 2. Of those that a mesh axis runs over, the one named last changes fastest.
Arguments:
- kernel: float32 [16384, 16384], P('row', 'col'), may hold values from -7 to 7, as said below
- nugget: float32 [16384], P('row'), may hold values from 0.25 to 1
Outputs:
- factored: float32 [16384, 16384], P('row', 'col')
Inputs may be any that keep to these rules, and one draw needn't show every extreme that they name: In matrix order the kernel is symmetric and positive semidefinite.
All inputs are finite; a program needn't handle non-finite values.
Results may differ from a plain program's by a relative error of at most 0.0018.
Values may be sent and summed in bfloat16 or wider, within the bound.
No kernel may reach another device: no remote copies, remote signals or barrier semaphores. Data moves between devices by JAX's collectives and lax.ppermute only.
A program may use at most 192 MiB of HBM per device.

v0:
```python
import jax
import jax.numpy as jnp
from jax import lax
from jax.sharding import PartitionSpec as P

B = 256
STEPS = 7


def broadcast(value, axis, source):
    kept = jnp.where(lax.axis_index(axis) == source, value, 0).astype(value.dtype)
    return lax.psum(kept, axis)


def apply_step(columns, row_side, col_part, later_rows, at_rows, later_cols):
    product = jnp.dot(row_side, col_part.T, preferred_element_type=jnp.float32)
    reduced = jnp.where(later_rows[:, None] & later_cols[None, :], columns - product, columns)
    return jnp.where(at_rows[:, None] & later_cols[None, :], jnp.float32(0.0), reduced)


def update_range(matrix, row_side, col_side, later_rows, at_rows, later_cols):
    return apply_step(matrix, row_side, col_side, later_rows, at_rows, later_cols)


def body(kernel, nugget):
    rows_here, cols_here = kernel.shape
    tile_width = B
    grid_rows = lax.axis_size("row")
    grid_cols = lax.axis_size("col")
    row_pos = lax.axis_index("row")
    col_pos = lax.axis_index("col")
    row_tiles = rows_here // tile_width
    row_offsets = jnp.arange(rows_here, dtype=jnp.int32)
    col_offsets = jnp.arange(cols_here, dtype=jnp.int32)
    row_tile_of = row_offsets // tile_width * grid_rows + row_pos
    col_tile_of = col_offsets // tile_width * grid_cols + col_pos
    same_entry = (row_tile_of[:, None] == col_tile_of[None, :]) & (
        (row_offsets % tile_width)[:, None] == (col_offsets % tile_width)[None, :]
    )
    matrix = kernel + jnp.where(same_entry, nugget[:, None], jnp.float32(0.0))
    for panel_step in range(STEPS):
        root_row = panel_step % grid_rows
        root_col = panel_step % grid_cols
        row_slot = panel_step // grid_rows
        col_slot = panel_step // grid_cols
        panel_strip = matrix[:, col_slot * tile_width : (col_slot + 1) * tile_width]
        diag_local = panel_strip[row_slot * tile_width : (row_slot + 1) * tile_width]
        diag_tile = broadcast(diag_local, "row", root_row)
        factor = jnp.linalg.cholesky(diag_tile)
        solved = lax.linalg.triangular_solve(
            factor, panel_strip, left_side=False, lower=True, transpose_a=True
        )
        row_side = broadcast(solved.astype(jnp.bfloat16), "col", root_col)
        share_rows = rows_here // grid_cols
        own_share = lax.dynamic_slice_in_dim(row_side, col_pos * share_rows, share_rows, 0)
        gathered = lax.all_gather(own_share[None], "row", axis=0, tiled=True)
        grouped = gathered.reshape(grid_rows // grid_cols, grid_cols, 1, share_rows, tile_width)
        regrouped = lax.all_to_all(grouped, "col", split_axis=1, concat_axis=2, tiled=True)
        owners = regrouped.reshape(grid_rows // grid_cols, row_tiles, tile_width, tile_width)
        col_side = jnp.transpose(owners, (1, 0, 2, 3)).reshape(cols_here, tile_width)
        later_rows = row_tile_of > panel_step
        at_rows = row_tile_of == panel_step
        later_cols = col_tile_of > panel_step
        is_root = col_pos == root_col
        stacked_factor = jnp.tile(factor, (row_tiles, 1))
        panel_lo = col_slot * tile_width
        panel_hi = panel_lo + tile_width
        updated = update_range(matrix, row_side, col_side, later_rows, at_rows, later_cols)
        columns = updated[:, panel_lo:panel_hi]
        panel_value = jnp.where(
            later_rows[:, None], solved, jnp.where(at_rows[:, None], stacked_factor, columns)
        )
        matrix = updated.at[:, panel_lo:panel_hi].set(jnp.where(is_root, panel_value, columns))
    return matrix


def solution(mesh):
    return jax.shard_map(
        body,
        mesh=mesh,
        in_specs=(P("row", "col"), P("row")),
        out_specs=P("row", "col"),
        check_vma=False,
    )
```

profile of v0, /device:TPU:0, one launch (start us, length us, event | category | flops | bytes accessed | tf_op | source)
XLA Modules:
  0.0 2180.3 jit_solution(15238127030930392028)
XLA Ops:
  6.6 33.3 %copy.93 = f32[2048,4096]{0,1:T(8,128)} copy(f32[2048,4096]{1,0:T(8,128)} %param.19) | data formatting | bytes 67108864 | tf_op args[0]
  68.4 56.3 %all-reduce.16.cloned.1.call-done = f32[256,256]{0,1:T(8,128)} async-done(((f32[256,256]{0,1:T(8,128)}), f32[256,256]{0,1:T(8,128)}) %all-reduce.16.cloned.1.call-update) | async-done | bytes 262160 | tf_op jit(solution)/shard_map/psum | solution.py:12
  196.0 51.3 %all-reduce.18.cloned.1.call-done = bf16[2048,256]{0,1:T(8,128)(2,1)} async-done(((bf16[2048,256]{0,1:T(8,128)(2,1)}), bf16[2048,256]{0,1:T(8,128)(2,1)}) %all-reduce.18.cloned.1.call-update) | async-done | bytes 1048592 | tf_op jit(solution)/shard_map/psum | solution.py:12
  291.6 44.5 %all-to-all-done = bf16[2,4,1,512,256]{4,3,0,2,1:T(8,128)(2,1)S(1)} async-done(((bf16[2,4,1,512,256]{4,3,0,2,1:T(8,128)(2,1)}), bf16[2,4,1,512,256]{4,3,0,2,1:T(8,128)(2,1)S(1)}, u32[]{:S(2)}, u32[]{:S(2)}) %all-to-all-start) | async-done | bytes 2097184 | tf_op jit(solution)/shard_map/all_to_all | solution.py:58
  369.9 51.6 %all-reduce.20.cloned.1.call-done = f32[256,256]{0,1:T(8,128)} async-done(((f32[256,256]{0,1:T(8,128)}), f32[256,256]{0,1:T(8,128)}) %all-reduce.20.cloned.1.call-update) | async-done | bytes 262160 | tf_op jit(solution)/shard_map/psum | solution.py:12
  490.3 51.3 %all-reduce.22.cloned.1.call-done = bf16[2048,256]{0,1:T(8,128)(2,1)} async-done(((bf16[2048,256]{0,1:T(8,128)(2,1)}), bf16[2048,256]{0,1:T(8,128)(2,1)}) %all-reduce.22.cloned.1.call-update) | async-done | bytes 1048592 | tf_op jit(solution)/shard_map/psum | solution.py:12
  585.2 45.1 %all-to-all-done.1 = bf16[2,4,1,512,256]{4,3,0,2,1:T(8,128)(2,1)S(1)} async-done(((bf16[2,4,1,512,256]{4,3,0,2,1:T(8,128)(2,1)}), bf16[2,4,1,512,256]{4,3,0,2,1:T(8,128)(2,1)S(1)}, u32[]{:S(2)}, u32[]{:S(2)}) %all-to-all-start.1) | async-done | bytes 2097184 | tf_op jit(solution)/shard_map/all_to_all | solution.py:58
  664.1 51.6 %all-reduce.24.cloned.1.call-done = f32[256,256]{0,1:T(8,128)} async-done(((f32[256,256]{0,1:T(8,128)}), f32[256,256]{0,1:T(8,128)}) %all-reduce.24.cloned.1.call-update) | async-done | bytes 262160 | tf_op jit(solution)/shard_map/psum | solution.py:12
  784.3 51.3 %all-reduce.26.cloned.1.call-done = bf16[2048,256]{0,1:T(8,128)(2,1)} async-done(((bf16[2048,256]{0,1:T(8,128)(2,1)}), bf16[2048,256]{0,1:T(8,128)(2,1)}) %all-reduce.26.cloned.1.call-update) | async-done | bytes 1048592 | tf_op jit(solution)/shard_map/psum | solution.py:12
  837.3 27.8 %all-gather.19.cloned.1.call-done = bf16[4096,256]{0,1:T(8,128)(2,1)} async-done(((bf16[512,256]{0,1:T(8,128)(2,1)}), bf16[4096,256]{0,1:T(8,128)(2,1)}) %all-gather.19.cloned.1.call-update) | async-done | bytes 2097168 | tf_op jit(solution)/shard_map/all_gather | solution.py:56
  879.3 45.1 %all-to-all-done.2 = bf16[2,4,1,512,256]{4,3,0,2,1:T(8,128)(2,1)S(1)} async-done(((bf16[2,4,1,512,256]{4,3,0,2,1:T(8,128)(2,1)}), bf16[2,4,1,512,256]{4,3,0,2,1:T(8,128)(2,1)S(1)}, u32[]{:S(2)}, u32[]{:S(2)}) %all-to-all-start.2) | async-done | bytes 2097184 | tf_op jit(solution)/shard_map/all_to_all | solution.py:58
  958.4 51.4 %all-reduce.28.cloned.1.call-done = f32[256,256]{0,1:T(8,128)} async-done(((f32[256,256]{0,1:T(8,128)}), f32[256,256]{0,1:T(8,128)}) %all-reduce.28.cloned.1.call-update) | async-done | bytes 262160 | tf_op jit(solution)/shard_map/psum | solution.py:12
  1077.1 51.3 %all-reduce.30.cloned.1.call-done = bf16[2048,256]{0,1:T(8,128)(2,1)} async-done(((bf16[2048,256]{0,1:T(8,128)(2,1)}), bf16[2048,256]{0,1:T(8,128)(2,1)}) %all-reduce.30.cloned.1.call-update) | async-done | bytes 1048592 | tf_op jit(solution)/shard_map/psum | solution.py:12
  1173.9 46.3 %all-to-all-done.3 = bf16[2,4,1,512,256]{4,3,0,2,1:T(8,128)(2,1)} async-done(((bf16[2,4,1,512,256]{4,3,0,2,1:T(8,128)(2,1)}), bf16[2,4,1,512,256]{4,3,0,2,1:T(8,128)(2,1)}, u32[]{:S(2)}, u32[]{:S(2)}) %all-to-all-start.3) | async-done | bytes 2097184 | tf_op jit(solution)/shard_map/all_to_all | solution.py:58
  1255.7 51.6 %all-reduce.32.cloned.1.call-done = f32[256,256]{0,1:T(8,128)} async-done(((f32[256,256]{0,1:T(8,128)}), f32[256,256]{0,1:T(8,128)}) %all-reduce.32.cloned.1.call-update) | async-done | bytes 262160 | tf_op jit(solution)/shard_map/psum | solution.py:12
  1378.7 51.3 %all-reduce.34.cloned.1.call-done = bf16[2048,256]{0,1:T(8,128)(2,1)} async-done(((bf16[2048,256]{0,1:T(8,128)(2,1)}), bf16[2048,256]{0,1:T(8,128)(2,1)}) %all-reduce.34.cloned.1.call-update) | async-done | bytes 1048592 | tf_op jit(solution)/shard_map/psum | solution.py:12
  1474.3 44.5 %all-to-all-done.4 = bf16[2,4,1,512,256]{4,3,0,2,1:T(8,128)(2,1)S(1)} async-done(((bf16[2,4,1,512,256]{4,3,0,2,1:T(8,128)(2,1)}), bf16[2,4,1,512,256]{4,3,0,2,1:T(8,128)(2,1)S(1)}, u32[]{:S(2)}, u32[]{:S(2)}) %all-to-all-start.4) | async-done | bytes 2097184 | tf_op jit(solution)/shard_map/all_to_all | solution.py:58
  1552.5 51.6 %all-reduce.36.cloned.1.call-done = f32[256,256]{0,1:T(8,128)} async-done(((f32[256,256]{0,1:T(8,128)}), f32[256,256]{0,1:T(8,128)}) %all-reduce.36.cloned.1.call-update) | async-done | bytes 262160 | tf_op jit(solution)/shard_map/psum | solution.py:12
  1672.7 51.3 %all-reduce.38.cloned.1.call-done = bf16[2048,256]{0,1:T(8,128)(2,1)} async-done(((bf16[2048,256]{0,1:T(8,128)(2,1)}), bf16[2048,256]{0,1:T(8,128)(2,1)}) %all-reduce.38.cloned.1.call-update) | async-done | bytes 1048592 | tf_op jit(solution)/shard_map/psum | solution.py:12
  1767.6 45.1 %all-to-all-done.5 = bf16[2,4,1,512,256]{4,3,0,2,1:T(8,128)(2,1)S(1)} async-done(((bf16[2,4,1,512,256]{4,3,0,2,1:T(8,128)(2,1)}), bf16[2,4,1,512,256]{4,3,0,2,1:T(8,128)(2,1)S(1)}, u32[]{:S(2)}, u32[]{:S(2)}) %all-to-all-start.5) | async-done | bytes 2097184 | tf_op jit(solution)/shard_map/all_to_all | solution.py:58
  1846.7 51.4 %all-reduce.40.cloned.1.call-done = f32[256,256]{0,1:T(8,128)} async-done(((f32[256,256]{0,1:T(8,128)}), f32[256,256]{0,1:T(8,128)}) %all-reduce.40.cloned.1.call-update) | async-done | bytes 262160 | tf_op jit(solution)/shard_map/psum | solution.py:12
  1965.5 51.3 %all-reduce.42.cloned.1.call-done = bf16[2048,256]{0,1:T(8,128)(2,1)} async-done(((bf16[2048,256]{0,1:T(8,128)(2,1)}), bf16[2048,256]{0,1:T(8,128)(2,1)}) %all-reduce.42.cloned.1.call-update) | async-done | bytes 1048592 | tf_op jit(solution)/shard_map/psum | solution.py:12
  2062.5 46.3 %all-to-all-done.6 = bf16[2,4,1,512,256]{4,3,0,2,1:T(8,128)(2,1)} async-done(((bf16[2,4,1,512,256]{4,3,0,2,1:T(8,128)(2,1)}), bf16[2,4,1,512,256]{4,3,0,2,1:T(8,128)(2,1)}, u32[]{:S(2)}, u32[]{:S(2)}) %all-to-all-start.6) | async-done | bytes 2097184 | tf_op jit(solution)/shard_map/all_to_all | solution.py:58
  2142.2 31.1 %copy.143 = f32[2048,4096]{1,0:T(8,128)} copy(f32[2048,4096]{0,1:T(8,128)} %fusion.8) | data formatting | bytes 67108864 | tf_op jit(solution)/shard_map/scatter | solution.py:73
  (388 shorter events, 1049.9 us)
Async XLA Ops:
  6.5 118.2 %all-reduce.16.cloned.1.call-start = ((), (), s32[]{:S(2)}) async-start(), calls=%async_computation.7 | async-start | bytes 524288 | tf_op jit(solution)/shard_map/psum | solution.py:12
  68.4 178.9 %all-reduce.18.cloned.1.call-start = ((), (), s32[]{:S(2)}) async-start(), calls=%async_computation.8 | async-start | bytes 2097152 | tf_op jit(solution)/shard_map/psum | solution.py:12
  196.0 80.9 %all-gather.15.cloned.1.call-start = ((), (), s32[]{:S(2)}) async-start(), calls=%async_computation.21 | async-start | bytes 2359296 | tf_op jit(solution)/shard_map/all_gather | solution.py:56
  282.9 53.2 %all-to-all-start = ((bf16[2,4,1,512,256]{4,3,0,2,1:T(8,128)(2,1)}), bf16[2,4,1,512,256]{4,3,0,2,1:T(8,128)(2,1)S(1)}, u32[]{:S(2)}, u32[]{:S(2)}) async-start(bf16[2,4,1,512,256]{4,3,0,2,1:T(8,128)(2,1)} %copy.96), calls=%async_computation | async-start | bytes 4194304 | tf_op jit(solution)/shard_map/all_to_all | solution.py:58
  287.5 134.0 %all-reduce.20.cloned.1.call-start = ((), (), s32[]{:S(2)}) async-start(), calls=%async_computation.9 | async-start | bytes 524288 | tf_op jit(solution)/shard_map/psum | solution.py:12
  369.6 171.9 %all-reduce.22.cloned.1.call-start = ((), (), s32[]{:S(2)}) async-start(), calls=%async_computation.10 | async-start | bytes 2097152 | tf_op jit(solution)/shard_map/psum | solution.py:12
  490.2 80.8 %all-gather.17.cloned.1.call-start = ((), (), s32[]{:S(2)}) async-start(), calls=%async_computation.22 | async-start | bytes 2359296 | tf_op jit(solution)/shard_map/all_gather | solution.py:56
  581.7 133.9 %all-reduce.24.cloned.1.call-start = ((), (), s32[]{:S(2)}) async-start(), calls=%async_computation.11 | async-start | bytes 524288 | tf_op jit(solution)/shard_map/psum | solution.py:12
  663.8 171.7 %all-reduce.26.cloned.1.call-start = ((), (), s32[]{:S(2)}) async-start(), calls=%async_computation.12 | async-start | bytes 2097152 | tf_op jit(solution)/shard_map/psum | solution.py:12
  784.2 80.8 %all-gather.19.cloned.1.call-start = ((), (), s32[]{:S(2)}) async-start(), calls=%async_computation.23 | async-start | bytes 2359296 | tf_op jit(solution)/shard_map/all_gather | solution.py:56
  875.8 134.0 %all-reduce.28.cloned.1.call-start = ((), (), s32[]{:S(2)}) async-start(), calls=%async_computation.13 | async-start | bytes 524288 | tf_op jit(solution)/shard_map/psum | solution.py:12
  957.9 170.5 %all-reduce.30.cloned.1.call-start = ((), (), s32[]{:S(2)}) async-start(), calls=%async_computation.14 | async-start | bytes 2097152 | tf_op jit(solution)/shard_map/psum | solution.py:12
  1077.0 80.8 %all-gather.21.cloned.1.call-start = ((), (), s32[]{:S(2)}) async-start(), calls=%async_computation.24 | async-start | bytes 2359296 | tf_op jit(solution)/shard_map/all_gather | solution.py:56
  1166.6 53.5 %all-to-all-start.3 = ((bf16[2,4,1,512,256]{4,3,0,2,1:T(8,128)(2,1)}), bf16[2,4,1,512,256]{4,3,0,2,1:T(8,128)(2,1)}, u32[]{:S(2)}, u32[]{:S(2)}) async-start(bf16[2,4,1,512,256]{4,3,0,2,1:T(8,128)(2,1)} %copy.117), calls=%async_computation.3 | async-start | bytes 4194304 | tf_op jit(solution)/shard_map/all_to_all | solution.py:58
  1171.4 135.9 %all-reduce.32.cloned.1.call-start = ((), (), s32[]{:S(2)}) async-start(), calls=%async_computation.15 | async-start | bytes 524288 | tf_op jit(solution)/shard_map/psum | solution.py:12
  1255.5 174.5 %all-reduce.34.cloned.1.call-start = ((), (), s32[]{:S(2)}) async-start(), calls=%async_computation.16 | async-start | bytes 2097152 | tf_op jit(solution)/shard_map/psum | solution.py:12
  1378.7 80.8 %all-gather.23.cloned.1.call-start = ((), (), s32[]{:S(2)}) async-start(), calls=%async_computation.25 | async-start | bytes 2359296 | tf_op jit(solution)/shard_map/all_gather | solution.py:56
  1470.1 133.9 %all-reduce.36.cloned.1.call-start = ((), (), s32[]{:S(2)}) async-start(), calls=%async_computation.17 | async-start | bytes 524288 | tf_op jit(solution)/shard_map/psum | solution.py:12
  1552.3 171.7 %all-reduce.38.cloned.1.call-start = ((), (), s32[]{:S(2)}) async-start(), calls=%async_computation.18 | async-start | bytes 2097152 | tf_op jit(solution)/shard_map/psum | solution.py:12
  1672.7 80.8 %all-gather.25.cloned.1.call-start = ((), (), s32[]{:S(2)}) async-start(), calls=%async_computation.26 | async-start | bytes 2359296 | tf_op jit(solution)/shard_map/all_gather | solution.py:56
  1764.2 133.9 %all-reduce.40.cloned.1.call-start = ((), (), s32[]{:S(2)}) async-start(), calls=%async_computation.19 | async-start | bytes 524288 | tf_op jit(solution)/shard_map/psum | solution.py:12
  1846.3 170.5 %all-reduce.42.cloned.1.call-start = ((), (), s32[]{:S(2)}) async-start(), calls=%async_computation.20 | async-start | bytes 2097152 | tf_op jit(solution)/shard_map/psum | solution.py:12
  1965.5 80.8 %all-gather.27.cloned.1.call-start = ((), (), s32[]{:S(2)}) async-start(), calls=%async_computation.27 | async-start | bytes 2359296 | tf_op jit(solution)/shard_map/all_gather | solution.py:56
  2055.1 53.8 %all-to-all-start.6 = ((bf16[2,4,1,512,256]{4,3,0,2,1:T(8,128)(2,1)}), bf16[2,4,1,512,256]{4,3,0,2,1:T(8,128)(2,1)}, u32[]{:S(2)}, u32[]{:S(2)}) async-start(bf16[2,4,1,512,256]{4,3,0,2,1:T(8,128)(2,1)} %copy.138), calls=%async_computation.6 | async-start | bytes 4194304 | tf_op jit(solution)/shard_map/all_to_all | solution.py:58
  (27 other events, 466.4 us)
Sparse Core Ops, SparseCore 0:
  68.5 56.2 all-reduce.15
  196.1 51.1 all-reduce.17
  249.2 27.5 all-gather.14
  369.8 51.6 all-reduce.19
  490.3 51.1 all-reduce.21
  543.4 27.5 all-gather.16
  664.0 51.6 all-reduce.23
  784.3 51.1 all-reduce.25
  837.5 27.5 all-gather.18
  958.0 51.6 all-reduce.27
  1077.2 51.1 all-reduce.29
  1130.2 27.5 all-gather.20
  1255.6 51.6 all-reduce.31
  1378.8 51.2 all-reduce.33
  1431.8 27.5 all-gather.22
  1552.4 51.6 all-reduce.35
  1672.8 51.1 all-reduce.37
  1725.8 27.5 all-gather.24
  1846.4 51.6 all-reduce.39
  1965.6 51.1 all-reduce.41
  2018.7 27.5 all-gather.26
where the time goes:
time: 2190 us; the launch traced here: 2180 us
  waiting for transfers between devices  1240 us (57%)
  other arithmetic  457 us (21%)
  matrix products  216 us (10%)
  local copies, waits for them, and re-layouts  211 us (10%)
  starting transfers between devices  34.8 us (2%)
  between operations  24 us (1%)
    psum x14, waiting for transfers between devices, broadcast(): return lax.psum(kept, axis)  724 us
    all_to_all x7, waiting for transfers between devices, body(): lax.all_to_all(grouped, 'col', split_axis=1, concat_axis=2, tiled=True)  317 us
    another operation x49, other arithmetic, body(): factor = jnp.linalg.cholesky(diag_tile)  243 us
    all_gather x7, waiting for transfers between devices, body(): gathered = lax.all_gather(own_share[None], 'row', axis=0, tiled=True)  194 us
    dot_general x7, matrix products, apply_step(): product = jnp.dot(row_side, col_part.T, preferred_element_type=jnp.float32)  185 us
    another operation x15, other arithmetic, body(): lax.linalg.triangular_solve(factor, panel_strip, left_side=False, lower=T...  143 us
    unnamed x54, local copies, waits for them, and re-layouts  72.7 us
    reshape x14, local copies, waits for them, and re-layouts, body(): gathered.reshape(grid_rows // grid_cols, grid_cols, 1, share_rows, tile_w...  48 us
  transfers between devices with their start and end apart: 28, of which 28 were waited for; matrix products, arithmetic and copies ran while one was open for 1% of the time, Pallas kernels for 0%

commit v1 on v0

v1 whole, which is shorter than its diff:
```python
import functools

import jax
import jax.numpy as jnp
from jax import lax
from jax.experimental import pallas as pl
from jax.experimental.pallas import tpu as pltpu
from jax.sharding import PartitionSpec as P

B = 256
STEPS = 7
FIRST = 4
SUB = 64
VMEM_LIMIT = 56 * 1024 * 1024


def assign_tiles(grid_cols):
    spare = STEPS
    sent, taken = {}, {}
    options = {}
    for a in range(STEPS):
        for b in range(a, STEPS):
            if b == a + grid_cols:
                sent[(a, b)] = (spare, a % grid_cols, 1, False)
                continue
            options[(a, b)] = [(a, b % grid_cols, b // grid_cols, False)]
            if a != b:
                options[(a, b)].append((b, a % grid_cols, a // grid_cols, True))

    def place(pair, seen):
        for option in options[pair]:
            device = option[:2]
            if device in seen:
                continue
            seen.add(device)
            if device not in taken or place(taken[device], seen):
                taken[device] = pair
                sent[pair] = option
                return True
        return False

    for pair in options:
        assert place(pair, set())
    return sent


def split(x):
    hi = x.astype(jnp.bfloat16)
    return hi, (x - hi.astype(jnp.float32)).astype(jnp.bfloat16)


def dot(a, b, dims=(1, 0)):
    return lax.dot_general(a, b, (((dims[0],), (dims[1],)), ((), ())), preferred_element_type=jnp.float32)


def dot_wide(a, b, dims=(1, 0)):
    a_hi, a_lo = split(a)
    b_hi, b_lo = split(b)
    return dot(a_hi, b_hi, dims) + (dot(a_hi, b_lo, dims) + dot(a_lo, b_hi, dims))


def eliminate(block):
    width = block.shape[1]
    count = SUB // 8
    rows = [block[8 * v : 8 * v + 8] for v in range(count)]
    sublane = lax.broadcasted_iota(jnp.int32, (8, width), 0)

    def lane(x, at):
        return jnp.broadcast_to(x[:, at : at + 1], (8, width))

    def row(x, at):
        return jnp.broadcast_to(x[at : at + 1], (8, width))

    for g in range(count):
        cols = [[lane(rows[v], 8 * g + m) for v in range(g, count)] for m in range(8)]
        pivot = {(a, b): row(cols[b][0], a) for b in range(8) for a in range(b, 8)}
        root, low = [None] * 8, {}
        for b in range(8):
            root[b] = lax.rsqrt(pivot[b, b])
            for a in range(b + 1, 8):
                low[a, b] = pivot[a, b] * root[b]
            for a in range(b + 1, 8):
                for c in range(b + 1, a + 1):
                    pivot[a, c] = pivot[a, c] - low[a, b] * low[c, b]
        inv = {}
        for b in range(8):
            inv[b, b] = root[b]
            for a in range(b + 1, 8):
                total = low[a, b] * inv[b, b]
                for m in range(b + 1, a):
                    total = total + low[a, m] * inv[m, b]
                inv[a, b] = -root[a] * total
        solved = None
        for b in range(8):
            coef = jnp.zeros((8, width), jnp.float32)
            for a in range(b, 8):
                coef = jnp.where(sublane == a, inv[a, b], coef)
            term = coef * row(rows[g], b)
            solved = term if solved is None else solved + term
        rows[g] = solved
        if g + 1 < count:
            across = [row(solved, m) for m in range(8)]
            for v in range(g + 1, count):
                total = None
                for m in range(8):
                    factor = inv[m, 0] * cols[0][v - g]
                    for b in range(1, m + 1):
                        factor = factor + inv[m, b] * cols[b][v - g]
                    term = factor * across[m]
                    total = term if total is None else total + term
                rows[v] = rows[v] - total
    return jnp.concatenate(rows, axis=0)


def factor_tile(work):
    eye = (
        lax.broadcasted_iota(jnp.int32, (SUB, 2 * SUB), 0) + SUB
        == lax.broadcasted_iota(jnp.int32, (SUB, 2 * SUB), 1)
    ).astype(jnp.float32)
    left = lax.broadcasted_iota(jnp.int32, (SUB, 2 * SUB), 1) < SUB
    for b in range(B // SUB):
        at = b * SUB
        base = at // (2 * SUB) * (2 * SUB)
        odd = at != base
        pair = work[at : at + SUB, base : base + 2 * SUB]
        if odd:
            pair = pltpu.roll(pair, SUB, 1)
        done = eliminate(jnp.where(left, pair, eye))
        moved = pltpu.roll(done, SUB, 1)
        inverse = moved[:, :SUB]
        end = B + base + 2 * SUB
        solved = dot_wide(inverse, work[at : at + SUB, base:end])
        if at + SUB < B:
            padded = jnp.where(left, 0.0, done) if odd else jnp.where(left, moved, 0.0)
            below = dot_wide(work[at + SUB : B, base : base + 2 * SUB], padded, (1, 1))
            start = (at + SUB) // (2 * SUB) * (2 * SUB)
            work[at + SUB : B, start:end] -= dot_wide(below, solved[:, start - base :])
        work[at : at + SUB, base:end] = solved


def factor_body(tiles_of, count, steps, share, chunk, *refs):
    if tiles_of is None:
        held_ref, refs = refs[0], refs[1:]
    else:
        tiles_ref, wide_ref, refs = refs[0], refs[1], refs[2:]
    rest_ref = None
    if steps < count:
        rest_ref, refs = refs[0], refs[1:]
    col_ref, row_ref, lower_ref, held, panel, work = refs
    edge = count * B
    if tiles_of is None:
        held[...] = held_ref[...]
    else:
        for (a, b), (index, turned) in tiles_of.items():
            tile = tiles_ref[index]
            held[a, :, b * B : (b + 1) * B] = tile.T if turned else tile
        for a in range(count):
            held[a, :, edge:] = wide_ref[a]
    above = lax.broadcasted_iota(jnp.int32, (B, B), 0)
    beside = lax.broadcasted_iota(jnp.int32, (B, B), 1)

    def step(k, carry):
        at = pl.multiple_of(k * B, B)
        work[:, :B] = held[k, :, pl.ds(at, B)]
        work[:, B:] = (above == beside).astype(jnp.float32)
        factor_tile(work)
        lower_ref[k] = jnp.where(above >= beside, work[:, :B].T, 0.0)
        inv_hi, inv_lo = split(work[:, B:])

        def solve(c, carry):
            where = pl.ds(pl.multiple_of(c * chunk, chunk), chunk)
            hi, lo = split(held[k, :, where])
            panel[:, where] = (dot(inv_hi, hi) + (dot(inv_hi, lo) + dot(inv_lo, hi))).astype(jnp.bfloat16)
            return carry

        lax.fori_loop((k + 1) * (B // chunk), (edge + share) // chunk, solve, 0)
        own = panel[:, edge:]
        col_ref[pl.ds(at, B), :] = own
        row_ref[:, pl.ds(at, B)] = own.T

        def reduce(i, carry):
            side = panel[:, pl.ds(pl.multiple_of(i * B, B), B)].T
            held[i] -= dot(side, panel[...])
            return carry

        lax.fori_loop(k + 1, count, reduce, 0)
        return carry

    panel[...] = jnp.zeros_like(panel)
    lax.fori_loop(0, steps, step, 0)
    if rest_ref is not None:
        rest_ref[...] = held[steps:, :, steps * B :]


def factor_group(operands, tiles_of, count, steps, share):
    chunk = min(B, share)
    f32, bf16 = jnp.float32, jnp.bfloat16
    outs = [
        jax.ShapeDtypeStruct((steps * B, share), bf16),
        jax.ShapeDtypeStruct((share, steps * B), bf16),
        jax.ShapeDtypeStruct((steps, B, B), f32),
    ]
    if steps < count:
        left = count - steps
        outs.insert(0, jax.ShapeDtypeStruct((left, B, left * B + share), f32))
    whole = pl.BlockSpec(memory_space=pltpu.VMEM)
    return pl.pallas_call(
        functools.partial(factor_body, tiles_of, count, steps, share, chunk),
        out_shape=outs,
        in_specs=[whole] * len(operands),
        out_specs=[whole] * len(outs),
        scratch_shapes=[
            pltpu.VMEM((count, B, count * B + share), f32),
            pltpu.VMEM((B, count * B + share), bf16),
            pltpu.VMEM((B, 2 * B), f32),
        ],
        compiler_params=pltpu.CompilerParams(vmem_limit_bytes=VMEM_LIMIT),
        cost_estimate=pl.CostEstimate(
            flops=steps * 2 * 10**9, bytes_accessed=16 * 2**20, transcendentals=0
        ),
        name="factor",
    )(*operands)


def trail_body(last, grid_rows, grid_cols, slots, width, *refs):
    place, prev_ref, *sides, col_ref, lower_ref, nugget_ref, out_ref = refs
    row_pos, col_pos = place[0], place[1]
    share = sides[0].shape[0]
    skip = B // width if last else 0
    start = (pl.program_id(0) + skip) * width
    slot, inner = start // B, pl.multiple_of(start % B, width)

    def rows_of(d):
        return pl.ds(pl.multiple_of(lax.rem(col_pos - d + grid_cols, grid_cols) * share, share), share)

    def product():
        for d in range(grid_cols):
            out_ref[rows_of(d), :] = prev_ref[rows_of(d), :] - dot(sides[d][...], col_ref[0])

    def panel():
        at = pl.multiple_of(col_pos * B + inner, width)
        for d in range(grid_cols):
            out_ref[rows_of(d), :] = sides[d][:, pl.ds(at, width)].astype(jnp.float32)
        step = col_pos + (FIRST if last else 0)

        @pl.when(row_pos == step)
        def _():
            out_ref[:B, :] = lower_ref[:, pl.ds(inner, width)]

        @pl.when(row_pos < step)
        def _():
            out_ref[:B, :] = jnp.zeros((B, width), jnp.float32)

    if last:
        in_panel = (slot == 1) & (col_pos + FIRST < STEPS)
        pl.when(in_panel)(panel)

        @pl.when(jnp.logical_not(in_panel))
        def _():
            product()

            @pl.when(row_pos < STEPS)
            def _():
                out_ref[:B, :] = jnp.zeros((B, width), jnp.float32)

    else:
        pl.when(slot == 0)(panel)

        @pl.when(slot > 0)
        def _():
            product()
            offset = slot * grid_cols + col_pos - row_pos
            level = offset // grid_rows

            @pl.when((offset >= 0) & (lax.rem(offset, grid_rows) == 0) & (level < slots))
            def _():
                own = pl.ds(pl.multiple_of(level * B, B), B)
                same = lax.broadcasted_iota(jnp.int32, (B, width), 0) == (
                    lax.broadcasted_iota(jnp.int32, (B, width), 1) + inner
                )
                value = nugget_ref[level, :, pl.ds(inner, width)]
                out_ref[own, :] += jnp.where(same, value, 0.0)


def trail(place, prev, sides, cols, lower, nugget, last, grid_rows, grid_cols):
    rows_here, cols_here = prev.shape
    share, depth = sides[0].shape
    width = min(B, share)
    slots = rows_here // B
    group = grid_rows // grid_cols
    skip = B // width if last else 0

    def col_block(u, place):
        start = (u + skip) * width
        slot, inner = start // B, start % B
        at = slot // group * B + inner
        return (slot % group * grid_cols + at // share, 0, at % share // width)

    def own_block(u, place):
        return (0, u + skip)

    block = pl.BlockSpec((rows_here, width), own_block)
    side = pl.BlockSpec((share, depth), lambda u, place: (0, 0))
    return pl.pallas_call(
        functools.partial(trail_body, last, grid_rows, grid_cols, slots, width),
        out_shape=jax.ShapeDtypeStruct(prev.shape, jnp.float32),
        grid_spec=pltpu.PrefetchScalarGridSpec(
            num_scalar_prefetch=1,
            grid=(cols_here // width - skip,),
            in_specs=[block]
            + [side] * grid_cols
            + [
                pl.BlockSpec((1, depth, width), col_block),
                pl.BlockSpec((B, B), lambda u, place: (0, 0)),
                pl.BlockSpec((slots, 1, B), lambda u, place: (0, 0, 0)),
            ],
            out_specs=block,
        ),
        input_output_aliases={1: 0} if last else {},
        compiler_params=pltpu.CompilerParams(
            vmem_limit_bytes=VMEM_LIMIT, dimension_semantics=("arbitrary",)
        ),
        cost_estimate=pl.CostEstimate(
            flops=2 * rows_here * cols_here * depth,
            bytes_accessed=8 * rows_here * cols_here,
            transcendentals=0,
        ),
        name="trail",
    )(place, prev, *sides, cols, lower, nugget)


def body(kernel, nugget):
    rows_here, cols_here = kernel.shape
    grid_rows = lax.axis_size("row")
    grid_cols = lax.axis_size("col")
    row_pos = lax.axis_index("row")
    col_pos = lax.axis_index("col")
    group = grid_rows // grid_cols
    share = rows_here // grid_cols
    slots = rows_here // B
    axes = ("row", "col")
    place = jnp.stack([row_pos, col_pos]).astype(jnp.int32)

    sent = assign_tiles(grid_cols)
    picked = [[0] * grid_cols for _ in range(grid_rows)]
    for row, col, slot, _ in sent.values():
        picked[row][col] = slot if row < STEPS else 0
    near, far = kernel[:B, :B], kernel[:B, B : 2 * B]
    passed = lax.ppermute(
        far,
        axes,
        [(a * grid_cols + a % grid_cols, STEPS * grid_cols + a % grid_cols) for a in range(STEPS - grid_cols)],
    )
    pick = jnp.asarray(picked, jnp.int32)[row_pos, col_pos]
    mine = jnp.where(row_pos == STEPS, passed, jnp.where(pick == 1, far, near))
    on_diagonal = (row_pos < STEPS) & (row_pos == pick * grid_cols + col_pos)
    same = jnp.arange(B)[:, None] == jnp.arange(B)[None, :]
    mine = mine + jnp.where(on_diagonal & same, nugget[:B][:, None], jnp.float32(0.0))
    tiles = lax.all_gather(mine, axes, axis=0, tiled=False)[: (STEPS + 1) * grid_cols]
    tiles_of = {pair: (row * grid_cols + col, turned) for pair, (row, col, _, turned) in sent.items()}

    top = jnp.transpose(kernel[:B].reshape(B, slots, group, B), (2, 0, 1, 3))
    top = jnp.transpose(top.reshape(group, B, grid_cols, share), (0, 2, 1, 3)).reshape(grid_rows, B, share)
    wide = lax.all_to_all(top, "row", split_axis=0, concat_axis=0, tiled=True)

    def exchange(col_own, row_own):
        cols = lax.all_gather(col_own, "row", axis=0, tiled=False)
        sides = []
        for d in range(grid_cols):
            pairs = []
            for g in range(group):
                for c in range(grid_cols):
                    for q in range(grid_cols):
                        source = (g * grid_cols + c) * grid_cols + q
                        target = (g * grid_cols + q) * grid_cols + (c + d) % grid_cols
                        pairs.append((source, target))
            sides.append(lax.ppermute(row_own, axes, pairs))
        return sides, cols

    nugget_rows = nugget.reshape(slots, 1, B)
    rest, col_own, row_own, lower = factor_group((tiles, wide), tiles_of, STEPS, FIRST, share)
    sides, cols = exchange(col_own, row_own)
    col_own, row_own, lower_late = factor_group((rest,), None, STEPS - FIRST, STEPS - FIRST, share)
    sides_late, cols_late = exchange(col_own, row_own)
    at = lax.dynamic_index_in_dim(lower, col_pos, 0, keepdims=False)
    matrix = trail(place, kernel, sides, cols, at, nugget_rows, False, grid_rows, grid_cols)
    at = lax.dynamic_index_in_dim(lower_late, jnp.minimum(col_pos, STEPS - FIRST - 1), 0, keepdims=False)
    return trail(place, matrix, sides_late, cols_late, at, nugget_rows, True, grid_rows, grid_cols)


def solution(mesh):
    return jax.shard_map(
        body,
        mesh=mesh,
        in_specs=(P("row", "col"), P("row")),
        out_specs=P("row", "col"),
        check_vma=False,
    )
```

time: 2190 us -> 434 us (0.20)
  waiting for transfers between devices: 1240 us -> 20.9 us
  other arithmetic: 457 us -> 2.44 us
  matrix products: 216 us -> 0 us
  local copies, waits for them, and re-layouts: 211 us -> 26.4 us
  Pallas kernels: 0 us -> 172 us
  starting transfers between devices: 34.8 us -> 119 us
  blocking collectives: 0 us -> 76.1 us
    psum x14 -> x0, waiting for transfers between devices: 724 us -> none  [broadcast(): return lax.psum(kept, axis)]
    another operation x66 -> x1, other arithmetic: 387 us -> 0.62 us  [body(): place = jnp.stack([row_pos, col_pos]).astype(jnp.int32)]
    all_to_all x7 -> x0, waiting for transfers between devices: 317 us -> none  [body(): lax.all_to_all(grouped, 'col', split_axis=1, concat_axis=2, tiled=True)]
    all_gather x7 -> x3, waiting for transfers between devices: 194 us -> 3.95 us  [the longest x1 3.92 us: body(): lax.all_gather(mine, axes, axis=0, tiled=False)[:(STEPS + 1) * grid_cols]]
    dot_general x7 -> x0, matrix products: 185 us -> none  [apply_step(): product = jnp.dot(row_side, col_part.T, preferred_element_type=jnp.float32)]
    pallas_call x0 -> x4, Pallas kernels: none -> 172 us  [the longest x2 106 us: factor_group(): pl.pallas_call(functools.partial(factor_body, tiles_of, count, steps, sha...]
    ppermute x0 -> x9, starting transfers between devices: none -> 119 us  [the longest x8 113 us: exchange(): sides.append(lax.ppermute(row_own, axes, pairs))]
    all_to_all x0 -> x1, blocking collectives: none -> 76.1 us  [body(): wide = lax.all_to_all(top, 'row', split_axis=0, concat_axis=0, tiled=True)]
  transfers between devices with their start and end apart: 28 -> 12, of which waited for: 28 -> 4; matrix products, arithmetic and copies ran while one was open for 1% -> 6% of each run, Pallas kernels for 0% -> 17%
where the time goes in v1:
time: 434 us; the launch traced here: 432 us
  Pallas kernels  172 us (40%)
  starting transfers between devices  119 us (27%)
  blocking collectives  76.1 us (18%)
  local copies, waits for them, and re-layouts  26.4 us (6%)
  waiting for transfers between devices  20.9 us (5%)
  between operations  14.5 us (3%)
    ppermute x8, starting transfers between devices, exchange(): sides.append(lax.ppermute(row_own, axes, pairs))  113 us
    pallas_call x2, Pallas kernels, factor_group(): pl.pallas_call(functools.partial(factor_body, tiles_of, count, steps, sha...  106 us
    all_to_all x1, blocking collectives, body(): wide = lax.all_to_all(top, 'row', split_axis=0, concat_axis=0, tiled=True)  76.1 us
    pallas_call x2, Pallas kernels, trail(): pl.pallas_call(functools.partial(trail_body, last, grid_rows, grid_cols,...  65.9 us
    ppermute x8, waiting for transfers between devices, exchange(): sides.append(lax.ppermute(row_own, axes, pairs))  16.3 us
  transfers between devices with their start and end apart: 12, of which 4 were waited for; matrix products, arithmetic and copies ran while one was open for 6% of the time, Pallas kernels for 17%

profile of v1, /device:TPU:0, one launch (start us, length us, event | category | flops | bytes accessed | tf_op | source)
XLA Modules:
  0.0 431.5 jit_solution(13445345813856397571)
XLA Ops:
  6.5 1.0 slice.12
  7.5 5.3 %collective-permute-start = (f32[256,256]{1,0:T(8,128)S(1)}, f32[256,256]{1,0:T(8,128)S(1)}, u32[]{:S(2)}, u32[]{:S(2)}) collective-permute-start(f32[256,256]{1,0:T(8,128)S(1)} %slice.12), channel_id=1, source_target_pairs={{0,28},{5,29},{10,30}} | collective-permute-start | bytes 786440 | tf_op jit(solution)/shard_map/ppermute | solution.py:349
  12.8 1.3 dynamic_slice.11
  16.6 1.8 select_add_fusion
  18.5 4.7 %slice.15 = f32[256,4096]{1,0:T(8,128)} slice(f32[2048,4096]{1,0:T(8,128)} %refs_1_.1), slice={[0:256], [0:4096]} | slice | bytes 8388608 | tf_op jit(solution)/shard_map/slice | solution.py:362
  23.2 5.6 %copy.9 = f32[256,4096]{0,1:T(8,128)} copy(f32[256,4096]{1,0:T(8,128)} %slice.15) | data formatting | bytes 8388608
  28.8 4.6 %copy.7 = f32[2,256,8,256]{1,3,2,0:T(8,128)} copy(f32[2,256,8,256]{1,3,0,2:T(8,128)} %bitcast.19) | data formatting | bytes 8388608 | tf_op jit(solution)/shard_map/transpose | solution.py:362
  33.4 5.2 %copy.8 = f32[2,4,256,512]{3,2,1,0:T(8,128)} copy(f32[2,4,256,512]{2,3,1,0:T(8,128)} %bitcast.20) | data formatting | bytes 8388608 | tf_op jit(solution)/shard_map/transpose | solution.py:363
  38.7 76.1 %all_to_all.5.refs_1_ = f32[8,256,512]{2,1,0:T(8,128)} all-to-all(f32[8,256,512]{2,1,0:T(8,128)} %bitcast.21), channel_id=1, replica_groups=mesh['row'=8,'col'=4] {'row'}, dimensions={0} | all-to-all | bytes 8388608 | tf_op jit(solution)/shard_map/all_to_all | solution.py:364
  114.8 3.9 all-gather.7.cloned.1.call-done
  118.7 67.3 %factor.2 = (f32[3,256,1280]{2,1,0:T(8,128)}, bf16[1024,512]{1,0:T(8,128)(2,1)}, bf16[512,1024]{1,0:T(8,128)(2,1)}, f32[4,256,256]{2,1,0:T(8,128)}) custom-call(f32[32,256,256]{2,1,0:T(8,128)} %bitcast.26, f32[8,256,512]{2,1,0:T(8,128)} %all_to_all.5.refs_1_), custom_call_target="tpu_custom_call" | custom-call | flops 8000000000 | bytes 16777216 | tf_op jit(solution)/shard_map/factor/pallas_call | solution.py:207
  186.3 39.1 %factor.3 = (bf16[768,512]{1,0:T(8,128)(2,1)}, bf16[512,768]{1,0:T(8,128)(2,1)}, f32[3,256,256]{2,1,0:T(8,128)}) custom-call(f32[3,256,1280]{2,1,0:T(8,128)} %get-tuple-element.15.refs_0_), custom_call_target="tpu_custom_call" | custom-call | flops 6000000000 | bytes 16777216 | tf_op jit(solution)/shard_map/factor/pallas_call | solution.py:207
  225.4 1.8 collective-permute-start.4
  227.3 1.9 collective-permute-start.3
  229.9 9.5 %collective-permute-start.1 = (bf16[512,1024]{1,0:T(8,128)(2,1)}, bf16[512,1024]{1,0:T(8,128)(2,1)}, u32[]{:S(2)}, u32[]{:S(2)}) collective-permute-start(bf16[512,1024]{1,0:T(8,128)(2,1)} %get-tuple-element.12), channel_id=1, source_target_pairs={{0,0},{1,4},{2,8},{3,12},{4,1},{5,5},{6,9},{7,13},{8,2},{9,6},{10,... | collective-permute-start | bytes 3145736 | tf_op jit(solution)/shard_map/ppermute | solution.py:377
  240.0 1.7 dynamic-slice_bitcast_fusion.1.refs_7_
  241.7 1.7 dynamic-slice_bitcast_fusion.refs_7_
  243.4 6.7 %collective-permute-done.4.refs_5_ = bf16[512,1024]{1,0:T(8,128)(2,1)S(1)} collective-permute-done((bf16[512,1024]{1,0:T(8,128)(2,1)}, bf16[512,1024]{1,0:T(8,128)(2,1)S(1)}, u32[]{:S(2)}, u32[]{:S(2)}) %collective-permute-start.4) | collective-permute-done | bytes 1048608 | tf_op jit(solution)/shard_map/ppermute | solution.py:377
  250.0 26.6 %collective-permute-start.7 = (bf16[512,768]{1,0:T(8,128)(2,1)}, bf16[512,768]{1,0:T(8,128)(2,1)}, u32[]{:S(2)}, u32[]{:S(2)}) collective-permute-start(bf16[512,768]{1,0:T(8,128)(2,1)} %get-tuple-element.16), channel_id=1, source_target_pairs={{0,2},{1,6},{2,10},{3,14},{4,3},{5,7},{6,11},{7,15},{8,0},{9,4},{1... | collective-permute-start | bytes 2359304 | tf_op jit(solution)/shard_map/ppermute | solution.py:377
  276.7 9.6 %collective-permute-done.3.refs_4_ = bf16[512,1024]{1,0:T(8,128)(2,1)S(1)} collective-permute-done((bf16[512,1024]{1,0:T(8,128)(2,1)}, bf16[512,1024]{1,0:T(8,128)(2,1)S(1)}, u32[]{:S(2)}, u32[]{:S(2)}) %collective-permute-start.3) | collective-permute-done | bytes 1048608 | tf_op jit(solution)/shard_map/ppermute | solution.py:377
  286.3 65.3 %collective-permute-start.6 = (bf16[512,768]{1,0:T(8,128)(2,1)}, bf16[512,768]{1,0:T(8,128)(2,1)}, u32[]{:S(2)}, u32[]{:S(2)}) collective-permute-start(bf16[512,768]{1,0:T(8,128)(2,1)} %get-tuple-element.16), channel_id=1, source_target_pairs={{0,1},{1,5},{2,9},{3,13},{4,2},{5,6},{6,10},{7,14},{8,3},{9,7},{10... | collective-permute-start | bytes 2359304 | tf_op jit(solution)/shard_map/ppermute | solution.py:377
  351.6 7.5 %collective-permute-start.5 = (bf16[512,768]{1,0:T(8,128)(2,1)}, bf16[512,768]{1,0:T(8,128)(2,1)}, u32[]{:S(2)}, u32[]{:S(2)}) collective-permute-start(bf16[512,768]{1,0:T(8,128)(2,1)} %get-tuple-element.16), channel_id=1, source_target_pairs={{0,0},{1,4},{2,8},{3,12},{4,1},{5,5},{6,9},{7,13},{8,2},{9,6},{10,... | collective-permute-start | bytes 2359304 | tf_op jit(solution)/shard_map/ppermute | solution.py:377
  359.1 35.2 %trail.2.refs_1_ = f32[2048,4096]{1,0:T(8,128)} custom-call(s32[2]{0:T(128)} %pad_add_fusion.refs_0_, f32[2048,4096]{1,0:T(8,128)} %refs_1_.1, bf16[512,1024]{1,0:T(8,128)(2,1)} %collective-permute-done.1.refs_2_, bf16[512,1024]{1,0:T(8,128)(2,1)} %copy-done.2, bf16[512,1024]{1,0:T(8,128)(2,1)} %copy-done.1, bf16[512,1024]{1,0:T(8,128)(2,1)} %copy-done, ...), custom_call_target="tpu_custom_call" | custom-call | flops 17179869184 | bytes 67108864 | tf_op jit(solution)/shard_map/trail/pallas_call | solution.py:304
  394.3 30.7 %trail.3 = f32[2048,4096]{1,0:T(8,128)} custom-call(s32[2]{0:T(128)} %pad_add_fusion.refs_0_, f32[2048,4096]{1,0:T(8,128)} %trail.2.refs_1_, bf16[512,768]{1,0:T(8,128)(2,1)} %collective-permute-done.5.refs_2_, bf16[512,768]{1,0:T(8,128)(2,1)} %collective-permute-done.6.refs_3_, ...), custom_call_target="tpu_custom_call", output_to_operand_aliasing={{}: (1, {})} | custom-call | flops 12884901888 | bytes 67108864 | tf_op jit(solution)/shard_map/trail/pallas_call | solution.py:304
  (25 shorter events, 3.0 us)
Async XLA Ops:
  6.5 112.2 %all-gather.7.cloned.1.call-start = ((), (), s32[]{:S(2)}) async-start(), calls=%async_computation.1 | async-start | bytes 8650752 | tf_op jit(solution)/shard_map/all_gather | solution.py:359
  7.5 9.1 %collective-permute-start = (f32[256,256]{1,0:T(8,128)S(1)}, f32[256,256]{1,0:T(8,128)S(1)}, u32[]{:S(2)}, u32[]{:S(2)}) collective-permute-start(f32[256,256]{1,0:T(8,128)S(1)} %slice.12), channel_id=1, source_target_pairs={{0,28},{5,29},{10,30}} | collective-permute-start | bytes 786440 | tf_op jit(solution)/shard_map/ppermute | solution.py:349
  18.5 340.6 %all-gather.9.cloned.1.call-start = ((), (), s32[]{:S(2)}) async-start(), calls=%async_computation.2 | async-start | bytes 9437184 | tf_op jit(solution)/shard_map/all_gather | solution.py:367
  186.1 208.2 %all-gather.11.cloned.1.call-start = ((), (), s32[]{:S(2)}) async-start(), calls=%async_computation.3 | async-start | bytes 7077888 | tf_op jit(solution)/shard_map/all_gather | solution.py:367
  225.4 24.6 %collective-permute-start.4 = (bf16[512,1024]{1,0:T(8,128)(2,1)}, bf16[512,1024]{1,0:T(8,128)(2,1)S(1)}, u32[]{:S(2)}, u32[]{:S(2)}) collective-permute-start(bf16[512,1024]{1,0:T(8,128)(2,1)} %get-tuple-element.12), channel_id=1, source_target_pairs={{0,3},{1,7},{2,11},{3,15},{4,0},{5,4},{6,8},{7,12},{8,1},{9,5},{10... | collective-permute-start | bytes 3145736 | tf_op jit(solution)/shard_map/ppermute | solution.py:377
  227.3 59.0 %collective-permute-start.3 = (bf16[512,1024]{1,0:T(8,128)(2,1)}, bf16[512,1024]{1,0:T(8,128)(2,1)S(1)}, u32[]{:S(2)}, u32[]{:S(2)}) collective-permute-start(bf16[512,1024]{1,0:T(8,128)(2,1)} %get-tuple-element.12), channel_id=1, source_target_pairs={{0,2},{1,6},{2,10},{3,14},{4,3},{5,7},{6,11},{7,15},{8,0},{9,4},{1... | collective-permute-start | bytes 3145736 | tf_op jit(solution)/shard_map/ppermute | solution.py:377
  229.2 122.4 %collective-permute-start.2 = (bf16[512,1024]{1,0:T(8,128)(2,1)}, bf16[512,1024]{1,0:T(8,128)(2,1)S(1)}, u32[]{:S(2)}, u32[]{:S(2)}) collective-permute-start(bf16[512,1024]{1,0:T(8,128)(2,1)} %get-tuple-element.12), channel_id=1, source_target_pairs={{0,1},{1,5},{2,9},{3,13},{4,2},{5,6},{6,10},{7,14},{8,3},{9,7},{10... | collective-permute-start | bytes 3145736 | tf_op jit(solution)/shard_map/ppermute | solution.py:377
  229.9 129.1 %collective-permute-start.1 = (bf16[512,1024]{1,0:T(8,128)(2,1)}, bf16[512,1024]{1,0:T(8,128)(2,1)}, u32[]{:S(2)}, u32[]{:S(2)}) collective-permute-start(bf16[512,1024]{1,0:T(8,128)(2,1)} %get-tuple-element.12), channel_id=1, source_target_pairs={{0,0},{1,4},{2,8},{3,12},{4,1},{5,5},{6,9},{7,13},{8,2},{9,6},{10,... | collective-permute-start | bytes 3145736 | tf_op jit(solution)/shard_map/ppermute | solution.py:377
  240.0 154.2 %collective-permute-start.8 = (bf16[512,768]{1,0:T(8,128)(2,1)}, bf16[512,768]{1,0:T(8,128)(2,1)}, u32[]{:S(2)}, u32[]{:S(2)}) collective-permute-start(bf16[512,768]{1,0:T(8,128)(2,1)} %get-tuple-element.16), channel_id=1, source_target_pairs={{0,3},{1,7},{2,11},{3,15},{4,0},{5,4},{6,8},{7,12},{8,1},{9,5},{10... | collective-permute-start | bytes 2359304 | tf_op jit(solution)/shard_map/ppermute | solution.py:377
  250.0 109.0 %copy-start = (bf16[512,1024]{1,0:T(8,128)(2,1)}, bf16[512,1024]{1,0:T(8,128)(2,1)S(1)}, u32[]{:S(2)}) copy-start(bf16[512,1024]{1,0:T(8,128)(2,1)S(1)} %collective-permute-done.4.refs_5_) | copy-start | bytes 3145732
  250.0 144.2 %collective-permute-start.7 = (bf16[512,768]{1,0:T(8,128)(2,1)}, bf16[512,768]{1,0:T(8,128)(2,1)}, u32[]{:S(2)}, u32[]{:S(2)}) collective-permute-start(bf16[512,768]{1,0:T(8,128)(2,1)} %get-tuple-element.16), channel_id=1, source_target_pairs={{0,2},{1,6},{2,10},{3,14},{4,3},{5,7},{6,11},{7,15},{8,0},{9,4},{1... | collective-permute-start | bytes 2359304 | tf_op jit(solution)/shard_map/ppermute | solution.py:377
  286.3 72.8 %copy-start.1 = (bf16[512,1024]{1,0:T(8,128)(2,1)}, bf16[512,1024]{1,0:T(8,128)(2,1)S(1)}, u32[]{:S(2)}) copy-start(bf16[512,1024]{1,0:T(8,128)(2,1)S(1)} %collective-permute-done.3.refs_4_) | copy-start | bytes 3145732
  286.3 108.0 %collective-permute-start.6 = (bf16[512,768]{1,0:T(8,128)(2,1)}, bf16[512,768]{1,0:T(8,128)(2,1)}, u32[]{:S(2)}, u32[]{:S(2)}) collective-permute-start(bf16[512,768]{1,0:T(8,128)(2,1)} %get-tuple-element.16), channel_id=1, source_target_pairs={{0,1},{1,5},{2,9},{3,13},{4,2},{5,6},{6,10},{7,14},{8,3},{9,7},{10... | collective-permute-start | bytes 2359304 | tf_op jit(solution)/shard_map/ppermute | solution.py:377
  351.6 7.5 %copy-start.2 = (bf16[512,1024]{1,0:T(8,128)(2,1)}, bf16[512,1024]{1,0:T(8,128)(2,1)S(1)}, u32[]{:S(2)}) copy-start(bf16[512,1024]{1,0:T(8,128)(2,1)S(1)} %collective-permute-done.2.refs_3_) | copy-start | bytes 3145732
  351.6 42.7 %collective-permute-start.5 = (bf16[512,768]{1,0:T(8,128)(2,1)}, bf16[512,768]{1,0:T(8,128)(2,1)}, u32[]{:S(2)}, u32[]{:S(2)}) collective-permute-start(bf16[512,768]{1,0:T(8,128)(2,1)} %get-tuple-element.16), channel_id=1, source_target_pairs={{0,0},{1,4},{2,8},{3,12},{4,1},{5,5},{6,9},{7,13},{8,2},{9,6},{10,... | collective-permute-start | bytes 2359304 | tf_op jit(solution)/shard_map/ppermute | solution.py:377
Sparse Core Ops, SparseCore 0:
  18.6 100.0 all-gather.6
  186.2 82.8 all-gather.8
  270.9 72.0 all-gather.10
